TPU v7x, 32 devices: a whole 2x2x4 slice. The times are simulated.
32 devices in a mesh: blk: 8 (over z, y), grp: 4 (over x, core).
Axes of the slice: x: 2, y: 2, z: 4, core: 2. Of those that a mesh axis runs over, the one named last changes fastest.
Arguments:
- block_inverse: bfloat16 [64, 1024, 1024], P(('blk', 'grp')), may hold values from -5 to 5
- coupling_in: bfloat16 [64, 1024, 1536], P(('blk', 'grp')), may hold values from -0.046875 to 0.046875
- coupling_out: bfloat16 [64, 1536, 1024], P(('blk', 'grp')), may hold values from -0.15625 to 0.15625
- sensitivities: bfloat16 [64, 1024, 512], P(('blk', 'grp')), may hold values from -6 to 6
- border_rhs: bfloat16 [1536, 512], replicated, may hold values from -6 to 6
- border_inverse: bfloat16 [1536, 1536], P('blk'), may hold values from -5 to 5
Outputs:
- adjoint: bfloat16 [64, 1024, 512], P(('blk', 'grp'))
- border_part: bfloat16 [1536, 512], P('blk')
All inputs are finite; a program needn't handle non-finite values.
Results may differ from a plain program's by a relative error of at most 0.0067.
Values may be sent and summed in bfloat16 or wider, within the bound.
A program may use at most 128 MiB of HBM per device.

v0:
```python
import jax
import jax.numpy as jnp
from jax import lax
from jax.sharding import PartitionSpec as P


def body(block_inverse, coupling_in, coupling_out, sensitivities, border_rhs, border_inverse):
    forward_part = jnp.einsum(
        "bji,bjk->bik", block_inverse, sensitivities, preferred_element_type=jnp.float32
    )
    forward_half = forward_part.astype(jnp.bfloat16)
    row_count = border_inverse.shape[0]
    owner_index = lax.axis_index("blk")
    full_term = jnp.einsum(
        "bnm,bnk->mk", coupling_in, forward_half, preferred_element_type=jnp.float32
    )
    summed_all = lax.psum(full_term, ("blk", "grp"))
    residual_half = (border_rhs.astype(jnp.float32) - summed_all).astype(jnp.bfloat16)
    full_border = lax.dot_general(
        lax.all_gather(border_inverse, "blk", axis=0, tiled=True),
        residual_half,
        (((0,), (0,)), ((), ())),
        preferred_element_type=jnp.float32,
    ).astype(jnp.bfloat16)
    border_rows = lax.dynamic_slice_in_dim(full_border, owner_index * row_count, row_count, 0)
    pulled = jnp.einsum(
        "bmn,mk->bnk", coupling_out, full_border, preferred_element_type=jnp.float32
    ).astype(jnp.bfloat16)
    back_term = jnp.einsum(
        "bji,bjk->bik", block_inverse, pulled, preferred_element_type=jnp.float32
    )
    adjoint = (forward_part - back_term).astype(jnp.bfloat16)
    return (adjoint, border_rows)


def solution(mesh):
    in_specs = (
        P(("blk", "grp"), None, None),
        P(("blk", "grp"), None, None),
        P(("blk", "grp"), None, None),
        P(("blk", "grp"), None, None),
        P(),
        P("blk", None),
    )
    out_specs = (P(("blk", "grp"), None, None), P("blk", None))
    return jax.shard_map(body, mesh=mesh, in_specs=in_specs, out_specs=out_specs, check_vma=False)
```

profile of v0, /device:TPU:0, one launch (start us, length us, event | category | flops | bytes accessed | tf_op | source)
XLA Modules:
  0.0 236.0 jit_solution(18283202891576643093)
XLA Ops:
  8.0 0.0 copy-start
  8.0 0.0 all-reduce.2.cloned.1.call-start
  8.1 1.5 copy-done
  9.6 4.6 %fusion.10 = f32[2,1024,512]{2,1,0:T(8,128)S(1)} fusion(bf16[2,1024,1024]{2,1,0:T(8,128)(2,1)} %param.6, bf16[2,1024,512]{2,1,0:T(8,128)(2,1)S(1)} %copy-done), kind=kOutput, calls=%fused_computation.11 | convolution fusion | flops 2147483648 | bytes 10485760 | tf_op jit(solution)/shard_map/bji,bjk->bik/dot_general | solution.py:8
  14.2 0.0 copy-start.2
  14.2 2.0 copy-done.2
  16.2 8.0 %convolution_bitcast_fusion = f32[1536,512]{1,0:T(8,128)} fusion(bf16[2,1024,1536]{2,1,0:T(8,128)(2,1)} %param.7, f32[2,1024,512]{2,1,0:T(8,128)S(1)} %fusion.10), kind=kOutput, calls=%fused_computation.2 | convolution fusion | flops 3222274048 | bytes 13631488 | tf_op jit(solution)/shard_map/bnm,bnk->mk/dot_general | solution.py:14
  24.2 0.0 all-reduce.2.cloned.1.call-update
  24.2 0.2 all-gather.2.cloned.1.call-start
  24.4 0.3 all-gather.2.cloned.1.call-update
  24.8 182.7 %all-reduce.2.cloned.1.call-done = f32[1536,512]{1,0:T(8,128)} async-done(((f32[1536,512]{1,0:T(8,128)}), f32[1536,512]{1,0:T(8,128)}) %all-reduce.2.cloned.1.call-update) | async-done | bytes 3145744 | tf_op jit(solution)/shard_map/psum | solution.py:17
  207.5 0.0 all-gather.2.cloned.1.call-done
  207.5 6.4 %convolution_convert_fusion = bf16[512,1536]{1,0:T(8,128)(2,1)S(1)} fusion(bf16[1536,1536]{1,0:T(8,128)(2,1)} %all-gather.2.cloned.1.call-done, f32[1536,512]{1,0:T(8,128)} %all-reduce.2.cloned.1.call-done, bf16[1536,512]{1,0:T(8,128)(2,1)} %param.10), kind=kOutput, calls=%fused_computation.4 | convolution fusion | flops 2419064832 | bytes 11010048 | tf_op jit(solution)/shard_map/dot_general | solution.py:19
  213.9 0.0 copy-start.1
  213.9 1.1 copy-done.1
  215.1 0.1 dynamic-slice_bitcast_fusion
  215.2 0.8 copy.10
  216.0 12.5 %fusion = bf16[2,1024,512]{2,1,0:T(8,128)(2,1)} fusion(f32[2,1024,512]{2,1,0:T(8,128)} %copy-done.2, bf16[2,1024,1024]{2,1,0:T(8,128)(2,1)} %param.6, bf16[2,1536,1024]{2,1,0:T(8,128)(2,1)} %param.8, bf16[512,1536]{1,0:T(8,128)(2,1)} %copy-done.1), kind=kOutput, calls=%fused_computation.1 | convolution fusion | flops 5371854848 | bytes 18350080 | tf_op jit(solution)/shard_map/bji,bjk->bik/dot_general | solution.py:29
Async XLA Ops:
  8.0 1.6 copy-start
  8.0 199.4 %all-reduce.2.cloned.1.call-start = ((), (), s32[]{:S(2)}) async-start(), calls=%async_computation | async-start | bytes 6291456 | tf_op jit(solution)/shard_map/psum | solution.py:17
  14.2 2.0 copy-start.2
  24.2 183.3 %all-gather.2.cloned.1.call-start = ((), (), s32[]{:S(2)}) async-start(), calls=%async_computation.1 | async-start | bytes 5308416 | tf_op jit(solution)/shard_map/all_gather | solution.py:20
  213.9 1.2 copy-start.1
Sparse Core Ops, SparseCore 0:
  24.3 183.0 all-reduce.1
Sparse Core Ops, SparseCore 1:
  26.9 87.9 all-gather.1
where the time goes:
time: 236 us
  waiting for transfers between devices  183 us (78%)
  matrix products  31.6 us (13%)
  between operations  15.5 us (7%)
  local copies, waits for them, and re-layouts  5.65 us (2%)
    psum x1, waiting for transfers between devices, body(): summed_all = lax.psum(full_term, ('blk', 'grp'))  183 us
    dot_general x1, matrix products, body(): jnp.einsum('bji,bjk->bik', block_inverse, pulled, preferred_element_type=...  12.5 us
    dot_general x1, matrix products, body(): jnp.einsum('bnm,bnk->mk', coupling_in, forward_half, preferred_element_ty...  8 us
    dot_general x1, matrix products, body(): lax.dot_general(lax.all_gather(border_inverse, 'blk', axis=0, tiled=True)...  6.44 us
    unnamed x7, local copies, waits for them, and re-layouts  5.5 us
  transfers between devices with their start and end apart: 2, of which 1 were waited for; matrix products, arithmetic and copies ran while one was open for 0% of the time, Pallas kernels for 0%

commit v1 on v0

v1 whole, which is shorter than its diff:
```python
import functools

import jax
import jax.numpy as jnp
from jax import lax
from jax.experimental import pallas as pl
from jax.experimental.pallas import tpu as pltpu
from jax.sharding import PartitionSpec as P

MESH = pl.DeviceIdType.MESH


def bit_of(index, k):
    return lax.rem(lax.div(index, 1 << k), 2)


def partner_of(index, k):
    return index + (1 - 2 * bit_of(index, k)) * (1 << k)


def border_kernel(
    n_blk, n_grp, term_ref, rhs_ref, inv_ref, out_ref,
    fold_refs, land_refs, sum_slots, part_ref, part_slots,
    fold_send, fold_recv, sum_send, sum_recv, part_send, part_recv,
    rows_send, rows_recv, cols_send, cols_recv,
):
    b = lax.axis_index("blk")
    g = lax.axis_index("grp")
    link, cols = term_ref.shape
    rows = link // n_blk
    steps = n_grp.bit_length() - 1
    f32 = jnp.float32

    barrier = pltpu.get_barrier_semaphore()
    for k in range(steps):
        pl.semaphore_signal(barrier, inc=1, device_id=(b, partner_of(g, k)), device_id_type=MESH)
    for d in range(1, n_blk):
        pl.semaphore_signal(barrier, inc=1, device_id=(lax.rem(b + d, n_blk), g), device_id_type=MESH)
    pl.semaphore_wait(barrier, steps + n_blk - 1)

    def row_block(index):
        return pl.ds(pl.multiple_of(index * rows, rows), rows)

    source = term_ref
    base = 0
    bases = []
    for k in range(steps):
        half = cols >> (k + 1)
        bit = bit_of(g, k)
        keep = pl.ds(pl.multiple_of(bit * half, half), half)
        give = pl.ds(pl.multiple_of((1 - bit) * half, half), half)
        copy = pltpu.make_async_remote_copy(
            src_ref=source.at[:, give], dst_ref=land_refs[k],
            send_sem=fold_send.at[k], recv_sem=fold_recv.at[k],
            device_id=(b, partner_of(g, k)), device_id_type=MESH,
        )
        copy.start()
        copy.wait()
        fold_refs[k][...] = (
            source[:, keep].astype(f32) + land_refs[k][...].astype(f32)
        ).astype(jnp.bfloat16)
        bases.append(base)
        base = base + bit * half
        source = fold_refs[k]

    def scatter(src, slots, send, recv):
        copies = []
        for d in range(1, n_blk):
            peer = lax.rem(b + d, n_blk)
            copy = pltpu.make_async_remote_copy(
                src_ref=src.at[row_block(peer), :], dst_ref=slots.at[d - 1],
                send_sem=send.at[d - 1], recv_sem=recv.at[d - 1],
                device_id=(peer, g), device_id_type=MESH,
            )
            copy.start()
            copies.append(copy)
        total = src[row_block(b), :].astype(f32)
        for d in range(1, n_blk):
            copies[d - 1].wait()
            total = total + slots[d - 1].astype(f32)
        return total

    residual = rhs_ref[...].astype(f32) - scatter(source, sum_slots, sum_send, sum_recv)
    part_ref[...] = lax.dot_general(
        inv_ref[...], residual.astype(jnp.bfloat16),
        (((0,), (0,)), ((), ())), preferred_element_type=f32,
    ).astype(jnp.bfloat16)
    width = cols // n_grp
    mine = scatter(part_ref, part_slots, part_send, part_recv)
    own_cols = pl.ds(pl.multiple_of(base, width), width)
    out_ref[row_block(b), own_cols] = mine.astype(jnp.bfloat16)

    copies = []
    for d in range(1, n_blk):
        place = out_ref.at[row_block(b), own_cols]
        copy = pltpu.make_async_remote_copy(
            src_ref=place, dst_ref=place,
            send_sem=rows_send.at[d - 1], recv_sem=rows_recv.at[d - 1],
            device_id=(lax.rem(b + d, n_blk), g), device_id_type=MESH,
        )
        copy.start()
        copies.append(copy)
    for d in range(1, n_blk):
        place = out_ref.at[row_block(lax.rem(b + n_blk - d, n_blk)), own_cols]
        copies[d - 1].wait_send()
        pltpu.make_async_remote_copy(
            src_ref=place, dst_ref=place,
            send_sem=rows_send.at[d - 1], recv_sem=rows_recv.at[d - 1],
            device_id=(lax.rem(b + d, n_blk), g), device_id_type=MESH,
        ).wait_recv()
    for k in reversed(range(steps)):
        half = cols >> (k + 1)
        bit = bit_of(g, k)
        place = out_ref.at[:, pl.ds(pl.multiple_of(bases[k] + bit * half, half), half)]
        other = out_ref.at[:, pl.ds(pl.multiple_of(bases[k] + (1 - bit) * half, half), half)]
        copy = pltpu.make_async_remote_copy(
            src_ref=place, dst_ref=place,
            send_sem=cols_send.at[k], recv_sem=cols_recv.at[k],
            device_id=(b, partner_of(g, k)), device_id_type=MESH,
        )
        copy.start()
        copy.wait_send()
        pltpu.make_async_remote_copy(
            src_ref=other, dst_ref=other,
            send_sem=cols_send.at[k], recv_sem=cols_recv.at[k],
            device_id=(b, partner_of(g, k)), device_id_type=MESH,
        ).wait_recv()


def border_solve(n_blk, n_grp, term, rhs, inverse):
    link, cols = term.shape
    rows, width = link // n_blk, cols // n_grp
    steps = n_grp.bit_length() - 1
    bf16 = jnp.bfloat16
    halves = [pltpu.VMEM((link, cols >> (k + 1)), bf16) for k in range(steps)]
    slots = pltpu.VMEM((n_blk - 1, rows, width), bf16)
    dma = pltpu.SemaphoreType.DMA
    vmem = pl.BlockSpec(memory_space=pltpu.VMEM)
    return pl.pallas_call(
        functools.partial(border_kernel, n_blk, n_grp),
        out_shape=jax.ShapeDtypeStruct((link, cols), bf16),
        in_specs=[vmem] * 3,
        out_specs=vmem,
        scratch_shapes=[
            halves, list(halves), slots, pltpu.VMEM((link, width), bf16), slots,
            dma((steps,)), dma((steps,)),
            dma((n_blk - 1,)), dma((n_blk - 1,)),
            dma((n_blk - 1,)), dma((n_blk - 1,)),
            dma((n_blk - 1,)), dma((n_blk - 1,)),
            dma((steps,)), dma((steps,)),
        ],
        compiler_params=pltpu.CompilerParams(
            collective_id=0, has_side_effects=True, vmem_limit_bytes=32 * 1024 * 1024
        ),
    )(term, rhs, inverse)


def column_base(n_grp, cols):
    g = lax.axis_index("grp")
    base = 0
    for k in range(n_grp.bit_length() - 1):
        base = base + bit_of(g, k) * (cols >> (k + 1))
    return base


def body(n_blk, n_grp, block_inverse, coupling_in, coupling_out, sensitivities, border_rhs, border_inverse):
    bf16 = jnp.bfloat16
    forward_part = jnp.einsum(
        "bji,bjk->bik", block_inverse, sensitivities, preferred_element_type=jnp.float32
    )
    forward_half = forward_part.astype(bf16)
    row_count = border_inverse.shape[0]
    cols = border_rhs.shape[1]
    first_row = lax.axis_index("blk") * row_count
    rhs = lax.dynamic_slice(
        border_rhs, (first_row, column_base(n_grp, cols)), (row_count, cols // n_grp)
    )
    full_term = jnp.einsum(
        "bnm,bnk->mk", coupling_in, forward_half, preferred_element_type=jnp.float32
    ).astype(bf16)
    full_border = border_solve(n_blk, n_grp, full_term, rhs, border_inverse)
    border_rows = lax.dynamic_slice_in_dim(full_border, first_row, row_count, 0)
    pulled = jnp.einsum(
        "bmn,mk->bnk", coupling_out, full_border, preferred_element_type=jnp.float32
    ).astype(bf16)
    back_term = jnp.einsum(
        "bji,bjk->bik", block_inverse, pulled, preferred_element_type=jnp.float32
    )
    adjoint = (forward_part - back_term).astype(bf16)
    return (adjoint, border_rows)


def solution(mesh):
    in_specs = (
        P(("blk", "grp"), None, None),
        P(("blk", "grp"), None, None),
        P(("blk", "grp"), None, None),
        P(("blk", "grp"), None, None),
        P(),
        P("blk", None),
    )
    out_specs = (P(("blk", "grp"), None, None), P("blk", None))
    run = functools.partial(body, mesh.shape["blk"], mesh.shape["grp"])
    return jax.shard_map(run, mesh=mesh, in_specs=in_specs, out_specs=out_specs, check_vma=False)
```

time: 236 us -> 84.1 us (0.36)
  the two profiles are of different devices: /device:TPU:0 before, /device:TPU:29 now
where the time goes in v1:
time: 84.1 us; the launch traced here: 83.9 us
  Pallas kernels  58 us (69%)
  matrix products  20.8 us (25%)
  local copies, waits for them, and re-layouts  4.4 us (5%)
    pallas_call x1, Pallas kernels, border_solve(): pl.pallas_call(functools.partial(border_kernel, n_blk, n_grp), out_shape=...  58 us
    dot_general x1, matrix products, body(): jnp.einsum('bji,bjk->bik', block_inverse, pulled, preferred_element_type=...  12.6 us
    dot_general x1, matrix products, body(): jnp.einsum('bji,bjk->bik', block_inverse, sensitivities, preferred_elemen...  4.7 us
    dot_general x1, matrix products, body(): jnp.einsum('bnm,bnk->mk', coupling_in, forward_half, preferred_element_ty...  3.47 us
    unnamed x10, local copies, waits for them, and re-layouts  1.83 us

profile of v1, /device:TPU:29, one launch (start us, length us, event | category | flops | bytes accessed | tf_op | source)
XLA Modules:
  0.0 83.9 jit_solution(9364709812320916644)
XLA Ops:
  0.6 0.0 copy-start
  0.7 1.0 %dynamic_slice.6.rhs_ref = bf16[192,128]{1,0:T(8,128)(2,1)S(1)} dynamic-slice(bf16[1536,512]{1,0:T(8,128)(2,1)} %param.10, s32[]{:T(128)S(6)} %select_n.7, s32[]{:T(128)S(6)} %select_n.8), dynamic_slice_sizes={192,128} | dynamic-slice | bytes 98308 | tf_op jit(solution)/shard_map/dynamic_slice | solution.py:175
  1.6 0.6 copy-done
  2.3 0.0 copy-start.3
  2.3 4.7 %fusion.12 = f32[2,1024,512]{2,1,0:T(8,128)S(1)} fusion(bf16[2,1024,1024]{2,1,0:T(8,128)(2,1)} %param.6, bf16[2,1024,512]{2,1,0:T(8,128)(2,1)S(1)} %copy-done), kind=kOutput, calls=%fused_computation.11 | convolution fusion | flops 2147483648 | bytes 10485760 | tf_op jit(solution)/shard_map/bji,bjk->bik/dot_general | solution.py:168
  7.0 0.0 copy-done.3
  7.0 0.0 copy-start.4
  7.0 0.0 copy-start.2
  7.0 3.5 %fusion.2.term_ref = bf16[1536,512]{1,0:T(8,128)(2,1)S(1)} fusion(bf16[2,1024,1536]{2,1,0:T(8,128)(2,1)S(1)} %copy-done.3, f32[2,1024,512]{2,1,0:T(8,128)S(1)} %fusion.12), kind=kOutput, calls=%fused_computation.4 | convolution fusion | flops 3223060480 | bytes 12058624 | tf_op jit(solution)/shard_map/bnm,bnk->mk/dot_general | solution.py:178
  10.5 0.0 copy-done.4
  10.5 0.0 copy-done.2
  10.5 58.0 %shard_map.77 = bf16[1536,512]{1,0:T(8,128)(2,1)S(1)} custom-call(bf16[1536,512]{1,0:T(8,128)(2,1)S(1)} %fusion.2.term_ref, bf16[192,128]{1,0:T(8,128)(2,1)S(1)} %dynamic_slice.6.rhs_ref, bf16[192,1536]{1,0:T(8,128)(2,1)S(1)} %copy-done.2), custom_call_target="tpu_custom_call" | custom-call | tf_op jit(solution)/shard_map/pallas_call | solution.py:139
  68.5 0.0 copy-start.1
  68.5 1.2 %copy-done.1 = bf16[1536,512]{1,0:T(8,128)(2,1)} copy-done((bf16[1536,512]{1,0:T(8,128)(2,1)}, bf16[1536,512]{1,0:T(8,128)(2,1)S(1)}, u32[]{:S(2)}) %copy-start.1) | copy-done | bytes 1572888
  69.7 12.6 %fusion = bf16[2,1024,512]{2,1,0:T(8,128)(2,1)} fusion(f32[2,1024,512]{2,1,0:T(8,128)} %copy-done.4, bf16[2,1024,1024]{2,1,0:T(8,128)(2,1)} %param.6, bf16[2,1536,1024]{2,1,0:T(8,128)(2,1)} %param.8, bf16[1536,512]{1,0:T(8,128)(2,1)} %copy-done.1), kind=kOutput, calls=%fused_computation.1 | convolution fusion | flops 5371854848 | bytes 18350080 | tf_op jit(solution)/shard_map/bji,bjk->bik/dot_general | solution.py:186
  82.3 1.6 %constant_dynamic-slice_fusion = bf16[192,512]{1,0:T(8,128)(2,1)} fusion(bf16[1536,512]{1,0:T(8,128)(2,1)} %copy-done.1, s32[]{:T(128)S(6)} %select_n.7), kind=kLoop, calls=%fused_computation.10 | loop fusion | bytes 393220 | tf_op jit(solution)/shard_map/dynamic_slice | solution.py:182
Async XLA Ops:
  0.6 1.6 %copy-start = (bf16[2,1024,512]{2,1,0:T(8,128)(2,1)S(1)}, bf16[2,1024,512]{2,1,0:T(8,128)(2,1)}, u32[]{:S(2)}) copy-start(bf16[2,1024,512]{2,1,0:T(8,128)(2,1)} %param.9) | copy-start | bytes 6291460
  2.3 4.7 %copy-start.3 = (bf16[2,1024,1536]{2,1,0:T(8,128)(2,1)S(1)}, bf16[2,1024,1536]{2,1,0:T(8,128)(2,1)}, u32[]{:S(2)}) copy-start(bf16[2,1024,1536]{2,1,0:T(8,128)(2,1)} %param.7) | copy-start | bytes 18874372
  7.0 3.5 %copy-start.4 = (f32[2,1024,512]{2,1,0:T(8,128)}, f32[2,1024,512]{2,1,0:T(8,128)S(1)}, u32[]{:S(2)}) copy-start(f32[2,1024,512]{2,1,0:T(8,128)S(1)} %fusion.12) | copy-start | bytes 12582916
  7.0 3.5 %copy-start.2 = (bf16[192,1536]{1,0:T(8,128)(2,1)S(1)}, bf16[192,1536]{1,0:T(8,128)(2,1)}, u32[]{:S(2)}) copy-start(bf16[192,1536]{1,0:T(8,128)(2,1)} %inv_ref.1) | copy-start | bytes 1769476
  68.5 1.2 %copy-start.1 = (bf16[1536,512]{1,0:T(8,128)(2,1)}, bf16[1536,512]{1,0:T(8,128)(2,1)S(1)}, u32[]{:S(2)}) copy-start(bf16[1536,512]{1,0:T(8,128)(2,1)S(1)} %shard_map.77) | copy-start | bytes 4718596

commit v2 on v0

v2 whole, which is shorter than its diff:
```python
import functools

import jax
import jax.numpy as jnp
from jax import lax
from jax.experimental import pallas as pl
from jax.experimental.pallas import tpu as pltpu
from jax.sharding import PartitionSpec as P

MESH = pl.DeviceIdType.MESH


def bit_of(index, k):
    return lax.rem(lax.div(index, 1 << k), 2)


def partner_of(index, k):
    return index + (1 - 2 * bit_of(index, k)) * (1 << k)


def border_kernel(
    n_blk, n_grp, parts, flat_ref, rhs_ref, inv_ref, out_ref,
    fold_refs, land_refs, sum_slots, part_ref, part_slots, residual_ref,
    fold_send, fold_recv, sum_send, sum_recv, part_send, part_recv,
    rows_send, rows_recv, cols_send, cols_recv,
):
    b = lax.axis_index("blk")
    g = lax.axis_index("grp")
    link, cols = flat_ref.shape
    rows = link // n_blk
    term_ref = flat_ref.reshape(n_blk, rows, cols)
    piece = rows // parts
    width = cols // n_grp
    steps = n_grp.bit_length() - 1
    f32, bf16 = jnp.float32, jnp.bfloat16
    peers = [lax.rem(b + d, n_blk) for d in range(1, n_blk)]
    origins = [lax.rem(b + n_blk - d, n_blk) for d in range(1, n_blk)]
    partners = [partner_of(g, k) for k in range(steps)]
    bits = [bit_of(g, k) for k in range(steps)]

    barrier = pltpu.get_barrier_semaphore()
    for partner in partners:
        pl.semaphore_signal(barrier, inc=1, device_id=(b, partner), device_id_type=MESH)
    for peer in peers:
        pl.semaphore_signal(barrier, inc=1, device_id=(peer, g), device_id_type=MESH)
    pl.semaphore_wait(barrier, steps + n_blk - 1)

    def rows_of(s):
        return pl.ds(s * piece, piece)

    def columns(index, size, base=0):
        return pl.ds(pl.multiple_of(base + index * size, size), size)

    def send(src, dst, device, send_sem, recv_sem):
        copy = pltpu.make_async_remote_copy(
            src_ref=src, dst_ref=dst, send_sem=send_sem, recv_sem=recv_sem,
            device_id=device, device_id_type=MESH,
        )
        copy.start()
        return copy

    def start_fold(k, s):
        source = term_ref if k == 0 else fold_refs[k - 1]
        half = cols >> (k + 1)
        return send(
            source.at[:, rows_of(s), columns(1 - bits[k], half)],
            land_refs[k].at[:, rows_of(s), :],
            (b, partners[k]), fold_send.at[k, s], fold_recv.at[k, s],
        )

    def start_scatter(src, slots, sends, recvs, s):
        return [
            send(
                src.at[peer, rows_of(s), :], slots.at[i, rows_of(s), :],
                (peer, g), sends.at[i, s], recvs.at[i, s],
            )
            for i, peer in enumerate(peers)
        ]

    def finish_scatter(copies, src, slots, s):
        total = src[b, rows_of(s), :].astype(f32)
        for i, copy in enumerate(copies):
            copy.wait()
            total = total + slots[i, rows_of(s), :].astype(f32)
        return total

    folds = [start_fold(0, s) for s in range(parts)]
    for k in range(steps):
        source = term_ref if k == 0 else fold_refs[k - 1]
        later = []
        for s in range(parts):
            folds[s].wait()
            keep = columns(bits[k], cols >> (k + 1))
            fold_refs[k][:, rows_of(s), :] = (
                source[:, rows_of(s), keep].astype(f32) + land_refs[k][:, rows_of(s), :].astype(f32)
            ).astype(bf16)
            if k + 1 < steps:
                later.append(start_fold(k + 1, s))
            else:
                later.append(start_scatter(fold_refs[k], sum_slots, sum_send, sum_recv, s))
        folds = later
    for s in range(parts):
        total = finish_scatter(folds[s], fold_refs[steps - 1], sum_slots, s)
        residual_ref[rows_of(s), :] = (rhs_ref[rows_of(s), :].astype(f32) - total).astype(bf16)

    part = lax.dot_general(
        inv_ref[...], residual_ref[...], (((0,), (0,)), ((), ())), preferred_element_type=f32
    ).astype(bf16)
    part_ref[...] = part.reshape(part_ref.shape)

    scatters = [
        start_scatter(part_ref, part_slots, part_send, part_recv, s) for s in range(parts)
    ]
    bases = [0]
    for k in range(steps):
        bases.append(bases[k] + bits[k] * (cols >> (k + 1)))
    own = columns(0, width, bases[steps])
    gathers = []
    for s in range(parts):
        total = finish_scatter(scatters[s], part_ref, part_slots, s)
        out_ref[b, rows_of(s), own] = total.astype(bf16)
        place = out_ref.at[b, rows_of(s), own]
        gathers.append([
            send(place, place, (peer, g), rows_send.at[i, s], rows_recv.at[i, s])
            for i, peer in enumerate(peers)
        ])

    def arrived(place, device, send_sem, recv_sem):
        pltpu.make_async_remote_copy(
            src_ref=place, dst_ref=place, send_sem=send_sem, recv_sem=recv_sem,
            device_id=device, device_id_type=MESH,
        ).wait_recv()

    def start_unfold(k, s):
        half = cols >> (k + 1)
        place = out_ref.at[:, rows_of(s), columns(bits[k], half, bases[k])]
        return send(place, place, (b, partners[k]), cols_send.at[k, s], cols_recv.at[k, s])

    unfolds = []
    for s in range(parts):
        for i, origin in enumerate(origins):
            gathers[s][i].wait_send()
            arrived(
                out_ref.at[origin, rows_of(s), own], (peers[i], g),
                rows_send.at[i, s], rows_recv.at[i, s],
            )
        unfolds.append(start_unfold(steps - 1, s))
    for k in reversed(range(steps)):
        half = cols >> (k + 1)
        later = []
        for s in range(parts):
            unfolds[s].wait_send()
            arrived(
                out_ref.at[:, rows_of(s), columns(1 - bits[k], half, bases[k])],
                (b, partners[k]), cols_send.at[k, s], cols_recv.at[k, s],
            )
            if k > 0:
                later.append(start_unfold(k - 1, s))
        unfolds = later


def border_solve(n_blk, n_grp, term, rhs, inverse):
    link, cols = term.shape
    rows, width = link // n_blk, cols // n_grp
    steps = n_grp.bit_length() - 1
    parts = 3 if rows % 48 == 0 else 1
    bf16 = jnp.bfloat16
    halves = [pltpu.VMEM((n_blk, rows, cols >> (k + 1)), bf16) for k in range(steps)]
    slots = pltpu.VMEM((n_blk - 1, rows, width), bf16)
    dma = pltpu.SemaphoreType.DMA
    vmem = pl.BlockSpec(memory_space=pltpu.VMEM)
    out = pl.pallas_call(
        functools.partial(border_kernel, n_blk, n_grp, parts),
        out_shape=jax.ShapeDtypeStruct((n_blk, rows, cols), bf16),
        in_specs=[vmem] * 3,
        out_specs=vmem,
        scratch_shapes=[
            halves, list(halves), slots, pltpu.VMEM((n_blk, rows, width), bf16), slots,
            pltpu.VMEM((rows, width), bf16),
            dma((steps, parts)), dma((steps, parts)),
            dma((n_blk - 1, parts)), dma((n_blk - 1, parts)),
            dma((n_blk - 1, parts)), dma((n_blk - 1, parts)),
            dma((n_blk - 1, parts)), dma((n_blk - 1, parts)),
            dma((steps, parts)), dma((steps, parts)),
        ],
        compiler_params=pltpu.CompilerParams(
            collective_id=0, has_side_effects=True, vmem_limit_bytes=32 * 1024 * 1024
        ),
    )(term, rhs, inverse)
    return out.reshape(link, cols)


def column_base(n_grp, cols):
    g = lax.axis_index("grp")
    base = 0
    for k in range(n_grp.bit_length() - 1):
        base = base + bit_of(g, k) * (cols >> (k + 1))
    return base


def body(n_blk, n_grp, block_inverse, coupling_in, coupling_out, sensitivities, border_rhs, border_inverse):
    bf16 = jnp.bfloat16
    forward_part = jnp.einsum(
        "bji,bjk->bik", block_inverse, sensitivities, preferred_element_type=jnp.float32
    )
    forward_half = forward_part.astype(bf16)
    row_count = border_inverse.shape[0]
    cols = border_rhs.shape[1]
    first_row = lax.axis_index("blk") * row_count
    rhs = lax.dynamic_slice(
        border_rhs, (first_row, column_base(n_grp, cols)), (row_count, cols // n_grp)
    )
    full_term = jnp.einsum(
        "bnm,bnk->mk", coupling_in, forward_half, preferred_element_type=jnp.float32
    ).astype(bf16)
    full_border = border_solve(n_blk, n_grp, full_term, rhs, border_inverse)
    border_rows = lax.dynamic_slice_in_dim(full_border, first_row, row_count, 0)
    pulled = jnp.einsum(
        "bmn,mk->bnk", coupling_out, full_border, preferred_element_type=jnp.float32
    ).astype(bf16)
    back_term = jnp.einsum(
        "bji,bjk->bik", block_inverse, pulled, preferred_element_type=jnp.float32
    )
    adjoint = (forward_part - back_term).astype(bf16)
    return (adjoint, border_rows)


def solution(mesh):
    in_specs = (
        P(("blk", "grp"), None, None),
        P(("blk", "grp"), None, None),
        P(("blk", "grp"), None, None),
        P(("blk", "grp"), None, None),
        P(),
        P("blk", None),
    )
    out_specs = (P(("blk", "grp"), None, None), P("blk", None))
    run = functools.partial(body, mesh.shape["blk"], mesh.shape["grp"])
    return jax.shard_map(run, mesh=mesh, in_specs=in_specs, out_specs=out_specs, check_vma=False)
```

time: 236 us -> 73.8 us (0.31)
  waiting for transfers between devices: 183 us -> 0 us
  Pallas kernels: 0 us -> 47.7 us
  between operations: 15.5 us -> 0.73 us
  matrix products: 31.6 us -> 20.8 us
    psum x1 -> x0, waiting for transfers between devices: 183 us -> none  [body(): summed_all = lax.psum(full_term, ('blk', 'grp'))]
    pallas_call x0 -> x1, Pallas kernels: none -> 47.7 us  [border_solve(): pl.pallas_call(functools.partial(border_kernel, n_blk, n_grp, parts), out...]
    dot_general x1 -> x0, matrix products: 6.44 us -> none  [body(): lax.dot_general(lax.all_gather(border_inverse, 'blk', axis=0, tiled=True)...]
    dot_general x1, matrix products: 8 us -> 3.47 us  [body(): jnp.einsum('bnm,bnk->mk', coupling_in, forward_half, preferred_element_ty...]
    unnamed x7 -> x10, local copies, waits for them, and re-layouts: 5.5 us -> 1.83 us
    dynamic_slice x1 -> x2, local copies, waits for them, and re-layouts: 0.14 us -> 2.57 us  [the longest x1 1.62 us: body(): border_rows = lax.dynamic_slice_in_dim(full_border, first_row, row_count, 0)]
  transfers between devices with their start and end apart: 2 -> 0, of which waited for: 1 -> 0; matrix products, arithmetic and copies ran while one was open for 0% -> 0% of each run, Pallas kernels for 0% -> 0%
where the time goes in v2:
time: 73.8 us; the launch traced here: 73.6 us
  Pallas kernels  47.7 us (65%)
  matrix products  20.8 us (28%)
  local copies, waits for them, and re-layouts  4.4 us (6%)
    pallas_call x1, Pallas kernels, border_solve(): pl.pallas_call(functools.partial(border_kernel, n_blk, n_grp, parts), out...  47.7 us
    dot_general x1, matrix products, body(): jnp.einsum('bji,bjk->bik', block_inverse, pulled, preferred_element_type=...  12.6 us
    dot_general x1, matrix products, body(): jnp.einsum('bji,bjk->bik', block_inverse, sensitivities, preferred_elemen...  4.71 us
    dot_general x1, matrix products, body(): jnp.einsum('bnm,bnk->mk', coupling_in, forward_half, preferred_element_ty...  3.47 us
    unnamed x10, local copies, waits for them, and re-layouts  1.83 us
    dynamic_slice x1, local copies, waits for them, and re-layouts, body(): border_rows = lax.dynamic_slice_in_dim(full_border, first_row, row_count, 0)  1.62 us

profile of v2, /device:TPU:0, one launch (start us, length us, event | category | flops | bytes accessed | tf_op | source)
XLA Modules:
  0.0 73.6 jit_solution(8086068579605463011)
XLA Ops:
  0.6 0.0 copy-start
  0.7 1.0 %dynamic_slice.6.rhs_ref = bf16[192,128]{1,0:T(8,128)(2,1)S(1)} dynamic-slice(bf16[1536,512]{1,0:T(8,128)(2,1)} %param.10, s32[]{:T(128)S(6)} %select_n.7, s32[]{:T(128)S(6)} %select_n.8), dynamic_slice_sizes={192,128} | dynamic-slice | bytes 98308 | tf_op jit(solution)/shard_map/dynamic_slice | solution.py:210
  1.6 0.6 copy-done
  2.3 0.0 copy-start.3
  2.3 4.7 %fusion.8 = f32[2,1024,512]{2,1,0:T(8,128)S(1)} fusion(bf16[2,1024,1024]{2,1,0:T(8,128)(2,1)} %param.6, bf16[2,1024,512]{2,1,0:T(8,128)(2,1)S(1)} %copy-done), kind=kOutput, calls=%fused_computation.10 | convolution fusion | flops 2147483648 | bytes 10485760 | tf_op jit(solution)/shard_map/bji,bjk->bik/dot_general | solution.py:203
  7.0 0.0 copy-done.3
  7.0 0.0 copy-start.4
  7.0 0.0 copy-start.2
  7.0 3.5 %fusion.2.flat_ref = bf16[1536,512]{1,0:T(8,128)(2,1)S(1)} fusion(bf16[2,1024,1536]{2,1,0:T(8,128)(2,1)S(1)} %copy-done.3, f32[2,1024,512]{2,1,0:T(8,128)S(1)} %fusion.8), kind=kOutput, calls=%fused_computation.4 | convolution fusion | flops 3223060480 | bytes 12058624 | tf_op jit(solution)/shard_map/bnm,bnk->mk/dot_general | solution.py:213
  10.5 0.0 copy-done.4
  10.5 0.0 copy-done.2
  10.5 47.7 %shard_map.77 = bf16[8,192,512]{2,1,0:T(8,128)(2,1)S(1)} custom-call(bf16[1536,512]{1,0:T(8,128)(2,1)S(1)} %fusion.2.flat_ref, bf16[192,128]{1,0:T(8,128)(2,1)S(1)} %dynamic_slice.6.rhs_ref, bf16[192,1536]{1,0:T(8,128)(2,1)S(1)} %copy-done.2), custom_call_target="tpu_custom_call" | custom-call | tf_op jit(solution)/shard_map/pallas_call | solution.py:172
  58.2 0.0 copy-start.1
  58.2 1.2 %copy-done.1 = bf16[8,192,512]{2,1,0:T(8,128)(2,1)} copy-done((bf16[8,192,512]{2,1,0:T(8,128)(2,1)}, bf16[8,192,512]{2,1,0:T(8,128)(2,1)S(1)}, u32[]{:S(2)}) %copy-start.1) | copy-done | bytes 1572888
  59.4 12.6 %fusion = bf16[2,1024,512]{2,1,0:T(8,128)(2,1)} fusion(f32[2,1024,512]{2,1,0:T(8,128)} %copy-done.4, bf16[2,1024,1024]{2,1,0:T(8,128)(2,1)} %param.6, bf16[1536,512,1]{1,0,2:T(8,128)(2,1)} %bitcast.24, bf16[2,1536,1024]{2,1,0:T(8,128)(2,1)} %param.8), kind=kOutput, calls=%fused_computation.1 | convolution fusion | flops 5371854848 | bytes 18350080 | tf_op jit(solution)/shard_map/bji,bjk->bik/dot_general | solution.py:221
  72.0 1.6 %constant_dynamic-slice_fusion = bf16[192,512]{1,0:T(8,128)(2,1)} fusion(bf16[1536,512]{1,0:T(8,128)(2,1)} %bitcast.25, s32[]{:T(128)S(6)} %select_n.7), kind=kLoop, calls=%fused_computation.9 | loop fusion | bytes 393220 | tf_op jit(solution)/shard_map/dynamic_slice | solution.py:217
Async XLA Ops:
  0.6 1.6 %copy-start = (bf16[2,1024,512]{2,1,0:T(8,128)(2,1)S(1)}, bf16[2,1024,512]{2,1,0:T(8,128)(2,1)}, u32[]{:S(2)}) copy-start(bf16[2,1024,512]{2,1,0:T(8,128)(2,1)} %param.9) | copy-start | bytes 6291460
  2.3 4.7 %copy-start.3 = (bf16[2,1024,1536]{2,1,0:T(8,128)(2,1)S(1)}, bf16[2,1024,1536]{2,1,0:T(8,128)(2,1)}, u32[]{:S(2)}) copy-start(bf16[2,1024,1536]{2,1,0:T(8,128)(2,1)} %param.7) | copy-start | bytes 18874372
  7.0 3.5 %copy-start.4 = (f32[2,1024,512]{2,1,0:T(8,128)}, f32[2,1024,512]{2,1,0:T(8,128)S(1)}, u32[]{:S(2)}) copy-start(f32[2,1024,512]{2,1,0:T(8,128)S(1)} %fusion.8) | copy-start | bytes 12582916
  7.0 3.5 %copy-start.2 = (bf16[192,1536]{1,0:T(8,128)(2,1)S(1)}, bf16[192,1536]{1,0:T(8,128)(2,1)}, u32[]{:S(2)}) copy-start(bf16[192,1536]{1,0:T(8,128)(2,1)} %inv_ref.1) | copy-start | bytes 1769476
  58.2 1.2 %copy-start.1 = (bf16[8,192,512]{2,1,0:T(8,128)(2,1)}, bf16[8,192,512]{2,1,0:T(8,128)(2,1)S(1)}, u32[]{:S(2)}) copy-start(bf16[8,192,512]{2,1,0:T(8,128)(2,1)S(1)} %shard_map.77) | copy-start | bytes 4718596

commit v3 on v2

--- a/solution.py
+++ b/solution.py
@@ -19,8 +19,8 @@
 
 
 def border_kernel(
-    n_blk, n_grp, parts, flat_ref, rhs_ref, inv_ref, out_ref,
-    fold_refs, land_refs, sum_slots, part_ref, part_slots, residual_ref,
+    n_blk, n_grp, parts, flat_ref, rhs_hbm, inv_ref, out_ref,
+    fold_refs, land_refs, sum_slots, part_ref, part_slots, residual_ref, rhs_ref, rhs_sem,
     fold_send, fold_recv, sum_send, sum_recv, part_send, part_recv,
     rows_send, rows_recv, cols_send, cols_recv,
 ):
@@ -38,6 +38,16 @@
     partners = [partner_of(g, k) for k in range(steps)]
     bits = [bit_of(g, k) for k in range(steps)]
 
+    bases = [0]
+    for k in range(steps):
+        bases.append(bases[k] + bits[k] * (cols >> (k + 1)))
+    fetch = pltpu.make_async_copy(
+        rhs_hbm.at[pl.ds(pl.multiple_of(b * rows, rows), rows),
+                   pl.ds(pl.multiple_of(bases[steps], width), width)],
+        rhs_ref, rhs_sem,
+    )
+    fetch.start()
+
     barrier = pltpu.get_barrier_semaphore()
     for partner in partners:
         pl.semaphore_signal(barrier, inc=1, device_id=(b, partner), device_id_type=MESH)
@@ -99,6 +109,7 @@
             else:
                 later.append(start_scatter(fold_refs[k], sum_slots, sum_send, sum_recv, s))
         folds = later
+    fetch.wait()
     for s in range(parts):
         total = finish_scatter(folds[s], fold_refs[steps - 1], sum_slots, s)
         residual_ref[rows_of(s), :] = (rhs_ref[rows_of(s), :].astype(f32) - total).astype(bf16)
@@ -111,9 +122,6 @@
     scatters = [
         start_scatter(part_ref, part_slots, part_send, part_recv, s) for s in range(parts)
     ]
-    bases = [0]
-    for k in range(steps):
-        bases.append(bases[k] + bits[k] * (cols >> (k + 1)))
     own = columns(0, width, bases[steps])
     gathers = []
     for s in range(parts):
@@ -163,7 +171,7 @@
     link, cols = term.shape
     rows, width = link // n_blk, cols // n_grp
     steps = n_grp.bit_length() - 1
-    parts = 3 if rows % 48 == 0 else 1
+    parts = max(p for p in (1, 2, 3) if rows % (16 * p) == 0)
     bf16 = jnp.bfloat16
     halves = [pltpu.VMEM((n_blk, rows, cols >> (k + 1)), bf16) for k in range(steps)]
     slots = pltpu.VMEM((n_blk - 1, rows, width), bf16)
@@ -172,11 +180,11 @@
     out = pl.pallas_call(
         functools.partial(border_kernel, n_blk, n_grp, parts),
         out_shape=jax.ShapeDtypeStruct((n_blk, rows, cols), bf16),
-        in_specs=[vmem] * 3,
+        in_specs=[vmem, pl.BlockSpec(memory_space=pl.ANY), vmem],
         out_specs=vmem,
         scratch_shapes=[
             halves, list(halves), slots, pltpu.VMEM((n_blk, rows, width), bf16), slots,
-            pltpu.VMEM((rows, width), bf16),
+            pltpu.VMEM((rows, width), bf16), pltpu.VMEM((rows, width), bf16), dma,
             dma((steps, parts)), dma((steps, parts)),
             dma((n_blk - 1, parts)), dma((n_blk - 1, parts)),
             dma((n_blk - 1, parts)), dma((n_blk - 1, parts)),
@@ -184,18 +192,10 @@
             dma((steps, parts)), dma((steps, parts)),
         ],
         compiler_params=pltpu.CompilerParams(
-            collective_id=0, has_side_effects=True, vmem_limit_bytes=32 * 1024 * 1024
+            collective_id=0, has_side_effects=True, vmem_limit_bytes=12 * 1024 * 1024
         ),
     )(term, rhs, inverse)
     return out.reshape(link, cols)
-
-
-def column_base(n_grp, cols):
-    g = lax.axis_index("grp")
-    base = 0
-    for k in range(n_grp.bit_length() - 1):
-        base = base + bit_of(g, k) * (cols >> (k + 1))
-    return base
 
 
 def body(n_blk, n_grp, block_inverse, coupling_in, coupling_out, sensitivities, border_rhs, border_inverse):
@@ -205,19 +205,16 @@
     )
     forward_half = forward_part.astype(bf16)
     row_count = border_inverse.shape[0]
-    cols = border_rhs.shape[1]
     first_row = lax.axis_index("blk") * row_count
-    rhs = lax.dynamic_slice(
-        border_rhs, (first_row, column_base(n_grp, cols)), (row_count, cols // n_grp)
-    )
     full_term = jnp.einsum(
         "bnm,bnk->mk", coupling_in, forward_half, preferred_element_type=jnp.float32
     ).astype(bf16)
-    full_border = border_solve(n_blk, n_grp, full_term, rhs, border_inverse)
+    full_border = border_solve(n_blk, n_grp, full_term, border_rhs, border_inverse)
     border_rows = lax.dynamic_slice_in_dim(full_border, first_row, row_count, 0)
     pulled = jnp.einsum(
         "bmn,mk->bnk", coupling_out, full_border, preferred_element_type=jnp.float32
     ).astype(bf16)
+    pulled = lax.optimization_barrier(pulled)
     back_term = jnp.einsum(
         "bji,bjk->bik", block_inverse, pulled, preferred_element_type=jnp.float32
     )

time: 73.8 us -> 66.4 us (0.90)
  matrix products: 20.8 us -> 15.5 us
  local copies, waits for them, and re-layouts: 4.4 us -> 2.31 us
    dot_general x1, matrix products: 12.6 us -> 3.7 us  [body(): jnp.einsum('bji,bjk->bik', block_inverse, pulled, preferred_element_type=...]
    dot_general x0 -> x1, matrix products: none -> 3.65 us  [body(): jnp.einsum('bmn,mk->bnk', coupling_out, full_border, preferred_element_ty...]
    dynamic_slice x1 -> x0, local copies, waits for them, and re-layouts: 0.95 us -> none  [body(): lax.dynamic_slice(border_rhs, (first_row, column_base(n_grp, cols)), (row...]
    dynamic_slice x1, local copies, waits for them, and re-layouts: 1.62 us -> 0.7 us  [body(): border_rows = lax.dynamic_slice_in_dim(full_border, first_row, row_count, 0)]
    unnamed x10 -> x14, local copies, waits for them, and re-layouts: 1.83 us -> 1.62 us
where the time goes in v3:
time: 66.4 us; the launch traced here: 66.3 us
  Pallas kernels  47.7 us (72%)
  matrix products  15.5 us (23%)
  local copies, waits for them, and re-layouts  2.31 us (3%)
  between operations  0.73 us (1%)
    pallas_call x1, Pallas kernels, border_solve(): pl.pallas_call(functools.partial(border_kernel, n_blk, n_grp, parts), out...  47.7 us
    dot_general x1, matrix products, body(): jnp.einsum('bji,bjk->bik', block_inverse, sensitivities, preferred_elemen...  4.7 us
    dot_general x1, matrix products, body(): jnp.einsum('bji,bjk->bik', block_inverse, pulled, preferred_element_type=...  3.7 us
    dot_general x1, matrix products, body(): jnp.einsum('bmn,mk->bnk', coupling_out, full_border, preferred_element_ty...  3.65 us
    dot_general x1, matrix products, body(): jnp.einsum('bnm,bnk->mk', coupling_in, forward_half, preferred_element_ty...  3.46 us
    unnamed x14, local copies, waits for them, and re-layouts  1.62 us

profile of v3, /device:TPU:0, one launch (start us, length us, event | category | flops | bytes accessed | tf_op | source)
XLA Modules:
  0.0 66.3 jit_solution(5312371403792233936)
XLA Ops:
  0.6 0.0 copy-start
  0.7 1.6 %copy-done = bf16[2,1024,512]{2,1,0:T(8,128)(2,1)S(1)} copy-done((bf16[2,1024,512]{2,1,0:T(8,128)(2,1)S(1)}, bf16[2,1024,512]{2,1,0:T(8,128)(2,1)}, u32[]{:S(2)}) %copy-start) | copy-done | bytes 2097176
  2.2 0.0 copy-start.3
  2.2 0.0 slice-start
  2.2 4.7 %fusion.4 = f32[2,1024,512]{2,1,0:T(8,128)S(1)} fusion(bf16[2,1024,1024]{2,1,0:T(8,128)(2,1)} %param.6, bf16[2,1024,512]{2,1,0:T(8,128)(2,1)S(1)} %copy-done), kind=kOutput, calls=%fused_computation.8 | convolution fusion | flops 2147483648 | bytes 10485760 | tf_op jit(solution)/shard_map/bji,bjk->bik/dot_general | solution.py:203
  6.9 0.0 copy-done.3
  6.9 0.0 copy-start.1
  7.0 0.0 copy-start.2
  7.0 0.0 slice-start.1
  7.0 3.5 %fusion.2.flat_ref = bf16[1536,512]{1,0:T(8,128)(2,1)S(1)} fusion(bf16[2,1024,1536]{2,1,0:T(8,128)(2,1)S(1)} %copy-done.3, f32[2,1024,512]{2,1,0:T(8,128)S(1)} %fusion.4), kind=kOutput, calls=%fused_computation.4 | convolution fusion | flops 3223060480 | bytes 12058624 | tf_op jit(solution)/shard_map/bnm,bnk->mk/dot_general | solution.py:209
  10.5 0.0 copy-done.1
  10.5 0.0 copy-done.2
  10.5 47.7 %shard_map.77 = bf16[8,192,512]{2,1,0:T(8,128)(2,1)S(1)} custom-call(bf16[1536,512]{1,0:T(8,128)(2,1)S(1)} %fusion.2.flat_ref, bf16[1536,512]{1,0:T(8,128)(2,1)S(1)} %copy-done.1, bf16[192,1536]{1,0:T(8,128)(2,1)S(1)} %copy-done.2), custom_call_target="tpu_custom_call" | custom-call | tf_op jit(solution)/shard_map/pallas_call | solution.py:180
  58.2 0.7 %constant_dynamic-slice_fusion = bf16[192,512]{1,0:T(8,128)(2,1)} fusion(bf16[1536,512]{1,0:T(8,128)(2,1)S(1)} %bitcast.24, s32[]{:T(128)S(6)} %select_n.3), kind=kLoop, calls=%fused_computation.7 | loop fusion | bytes 393220 | tf_op jit(solution)/shard_map/dynamic_slice | solution.py:213
  58.9 0.0 slice-done
  58.9 0.0 slice-done.1
  58.9 0.0 copy-start.4
  58.9 3.7 %convert_bitcast_fusion = bf16[2,1024,512]{1,2,0:T(8,128)(2,1)S(1)} fusion(bf16[1536,512,1]{1,0,2:T(8,128)(2,1)S(1)} %bitcast.25, bf16[2,1536,1024]{2,1,0:T(8,128)(2,1)S(1)} %bitcast.27), kind=kOutput, calls=%fused_computation.5 | convolution fusion | flops 3222274048 | bytes 9961472 | tf_op jit(solution)/shard_map/bmn,mk->bnk/dot_general | solution.py:214
  62.6 0.0 copy-done.4
  62.6 3.7 %fusion = bf16[2,1024,512]{2,1,0:T(8,128)(2,1)} fusion(f32[2,1024,512]{2,1,0:T(8,128)S(1)} %fusion.4, bf16[2,1024,512]{1,2,0:T(8,128)(2,1)S(1)} %convert_bitcast_fusion, bf16[2,1024,1024]{2,1,0:T(8,128)(2,1)S(1)} %copy-done.4), kind=kOutput, calls=%fused_computation.1 | convolution fusion | flops 2149580800 | bytes 12582912 | tf_op jit(solution)/shard_map/bji,bjk->bik/dot_general | solution.py:218
  (1 shorter events, 0.0 us)
Async XLA Ops:
  0.6 1.6 %copy-start = (bf16[2,1024,512]{2,1,0:T(8,128)(2,1)S(1)}, bf16[2,1024,512]{2,1,0:T(8,128)(2,1)}, u32[]{:S(2)}) copy-start(bf16[2,1024,512]{2,1,0:T(8,128)(2,1)} %param.9) | copy-start | bytes 6291460
  2.2 4.7 %copy-start.3 = (bf16[2,1024,1536]{2,1,0:T(8,128)(2,1)S(1)}, bf16[2,1024,1536]{2,1,0:T(8,128)(2,1)}, u32[]{:S(2)}) copy-start(bf16[2,1024,1536]{2,1,0:T(8,128)(2,1)} %param.7) | copy-start | bytes 18874372
  2.2 56.7 %slice-start = ((s8[6291456]{0:T(1024)(128)(4,1)}), s8[4194304]{0:T(1024)(128)(4,1)S(1)}, s32[]{:S(2)}) async-start(s8[6291456]{0:T(1024)(128)(4,1)} %bitcast.26), calls=%async_computation | async-start | bytes 8388608
  6.9 3.5 %copy-start.1 = (bf16[1536,512]{1,0:T(8,128)(2,1)S(1)}, bf16[1536,512]{1,0:T(8,128)(2,1)}, u32[]{:S(2)}) copy-start(bf16[1536,512]{1,0:T(8,128)(2,1)} %rhs_hbm.1) | copy-start | bytes 4718596
  7.0 3.5 %copy-start.2 = (bf16[192,1536]{1,0:T(8,128)(2,1)S(1)}, bf16[192,1536]{1,0:T(8,128)(2,1)}, u32[]{:S(2)}) copy-start(bf16[192,1536]{1,0:T(8,128)(2,1)} %inv_ref.1) | copy-start | bytes 1769476
  7.0 51.9 %slice-start.1 = ((s8[6291456]{0:T(1024)(128)(4,1)}), s8[2097152]{0:T(1024)(128)(4,1)S(1)}, s32[]{:S(2)}) async-start(s8[6291456]{0:T(1024)(128)(4,1)} %bitcast.26), calls=%async_computation.1 | async-start | bytes 4194304
  58.9 3.7 %copy-start.4 = (bf16[2,1024,1024]{2,1,0:T(8,128)(2,1)S(1)}, bf16[2,1024,1024]{2,1,0:T(8,128)(2,1)}, u32[]{:S(2)}) copy-start(bf16[2,1024,1024]{2,1,0:T(8,128)(2,1)} %param.6) | copy-start | bytes 12582916

commit v4 on v3

--- a/solution.py
+++ b/solution.py
@@ -20,9 +20,9 @@
 
 def border_kernel(
     n_blk, n_grp, parts, flat_ref, rhs_hbm, inv_ref, out_ref,
-    fold_refs, land_refs, sum_slots, part_ref, part_slots, residual_ref, rhs_ref, rhs_sem,
+    fold_refs, land_refs, sum_slots, part_ref, pair_land, pair_ref, part_slots, residual_ref, rhs_ref, rhs_sem,
     fold_send, fold_recv, sum_send, sum_recv, part_send, part_recv,
-    rows_send, rows_recv, cols_send, cols_recv,
+    pair_send, pair_recv, rows_send, rows_recv, mate_send, mate_recv, cols_send, cols_recv,
 ):
     b = lax.axis_index("blk")
     g = lax.axis_index("grp")
@@ -34,7 +34,11 @@
     steps = n_grp.bit_length() - 1
     f32, bf16 = jnp.float32, jnp.bfloat16
     peers = [lax.rem(b + d, n_blk) for d in range(1, n_blk)]
-    origins = [lax.rem(b + n_blk - d, n_blk) for d in range(1, n_blk)]
+    pairs = n_blk // 2
+    side, pair = lax.rem(b, 2), lax.div(b, 2)
+    mate = b + 1 - 2 * side
+    near = [lax.rem(pair + d, pairs) for d in range(1, pairs)]
+    origins = [lax.rem(pair + pairs - d, pairs) for d in range(1, pairs)]
     partners = [partner_of(g, k) for k in range(steps)]
     bits = [bit_of(g, k) for k in range(steps)]
 
@@ -78,17 +82,17 @@
             (b, partners[k]), fold_send.at[k, s], fold_recv.at[k, s],
         )
 
-    def start_scatter(src, slots, sends, recvs, s):
+    def start_scatter(src, slots, sends, recvs, s, places, owners):
         return [
             send(
-                src.at[peer, rows_of(s), :], slots.at[i, rows_of(s), :],
-                (peer, g), sends.at[i, s], recvs.at[i, s],
+                src.at[place, rows_of(s), :], slots.at[i, rows_of(s), :],
+                (owner, g), sends.at[i, s], recvs.at[i, s],
             )
-            for i, peer in enumerate(peers)
+            for i, (place, owner) in enumerate(zip(places, owners))
         ]
 
-    def finish_scatter(copies, src, slots, s):
-        total = src[b, rows_of(s), :].astype(f32)
+    def finish_scatter(copies, src, slots, s, place):
+        total = src[place, rows_of(s), :].astype(f32)
         for i, copy in enumerate(copies):
             copy.wait()
             total = total + slots[i, rows_of(s), :].astype(f32)
@@ -107,11 +111,13 @@
             if k + 1 < steps:
                 later.append(start_fold(k + 1, s))
             else:
-                later.append(start_scatter(fold_refs[k], sum_slots, sum_send, sum_recv, s))
+                later.append(start_scatter(
+                    fold_refs[k], sum_slots, sum_send, sum_recv, s, peers, peers
+                ))
         folds = later
     fetch.wait()
     for s in range(parts):
-        total = finish_scatter(folds[s], fold_refs[steps - 1], sum_slots, s)
+        total = finish_scatter(folds[s], fold_refs[steps - 1], sum_slots, s, b)
         residual_ref[rows_of(s), :] = (rhs_ref[rows_of(s), :].astype(f32) - total).astype(bf16)
 
     part = lax.dot_general(
@@ -119,18 +125,32 @@
     ).astype(bf16)
     part_ref[...] = part.reshape(part_ref.shape)
 
-    scatters = [
-        start_scatter(part_ref, part_slots, part_send, part_recv, s) for s in range(parts)
+    owners = [place * 2 + side for place in near]
+    swaps = [
+        send(
+            part_ref.at[:, 1 - side, rows_of(s), :], pair_land.at[:, rows_of(s), :],
+            (mate, g), pair_send.at[s], pair_recv.at[s],
+        )
+        for s in range(parts)
     ]
+    scatters = []
+    for s in range(parts):
+        swaps[s].wait()
+        pair_ref[:, rows_of(s), :] = (
+            part_ref[:, side, rows_of(s), :].astype(f32) + pair_land[:, rows_of(s), :].astype(f32)
+        ).astype(bf16)
+        scatters.append(start_scatter(
+            pair_ref, part_slots, part_send, part_recv, s, near, owners
+        ))
     own = columns(0, width, bases[steps])
     gathers = []
     for s in range(parts):
-        total = finish_scatter(scatters[s], part_ref, part_slots, s)
-        out_ref[b, rows_of(s), own] = total.astype(bf16)
-        place = out_ref.at[b, rows_of(s), own]
+        total = finish_scatter(scatters[s], pair_ref, part_slots, s, pair)
+        out_ref[pair, side, rows_of(s), own] = total.astype(bf16)
+        place = out_ref.at[pair, side, rows_of(s), own]
         gathers.append([
-            send(place, place, (peer, g), rows_send.at[i, s], rows_recv.at[i, s])
-            for i, peer in enumerate(peers)
+            send(place, place, (owner, g), rows_send.at[i, s], rows_recv.at[i, s])
+            for i, owner in enumerate(owners)
         ])
 
     def arrived(place, device, send_sem, recv_sem):
@@ -141,17 +161,26 @@
 
     def start_unfold(k, s):
         half = cols >> (k + 1)
-        place = out_ref.at[:, rows_of(s), columns(bits[k], half, bases[k])]
+        place = out_ref.at[:, :, rows_of(s), columns(bits[k], half, bases[k])]
         return send(place, place, (b, partners[k]), cols_send.at[k, s], cols_recv.at[k, s])
 
-    unfolds = []
+    swaps = []
     for s in range(parts):
         for i, origin in enumerate(origins):
             gathers[s][i].wait_send()
             arrived(
-                out_ref.at[origin, rows_of(s), own], (peers[i], g),
+                out_ref.at[origin, side, rows_of(s), own], (owners[i], g),
                 rows_send.at[i, s], rows_recv.at[i, s],
             )
+        place = out_ref.at[:, side, rows_of(s), own]
+        swaps.append(send(place, place, (mate, g), mate_send.at[s], mate_recv.at[s]))
+    unfolds = []
+    for s in range(parts):
+        swaps[s].wait_send()
+        arrived(
+            out_ref.at[:, 1 - side, rows_of(s), own], (mate, g),
+            mate_send.at[s], mate_recv.at[s],
+        )
         unfolds.append(start_unfold(steps - 1, s))
     for k in reversed(range(steps)):
         half = cols >> (k + 1)
@@ -159,7 +188,7 @@
         for s in range(parts):
             unfolds[s].wait_send()
             arrived(
-                out_ref.at[:, rows_of(s), columns(1 - bits[k], half, bases[k])],
+                out_ref.at[:, :, rows_of(s), columns(1 - bits[k], half, bases[k])],
                 (b, partners[k]), cols_send.at[k, s], cols_recv.at[k, s],
             )
             if k > 0:
@@ -171,7 +200,7 @@
     link, cols = term.shape
     rows, width = link // n_blk, cols // n_grp
     steps = n_grp.bit_length() - 1
-    parts = max(p for p in (1, 2, 3) if rows % (16 * p) == 0)
+    parts = max(p for p in (1, 2, 3, 4) if rows % (16 * p) == 0)
     bf16 = jnp.bfloat16
     halves = [pltpu.VMEM((n_blk, rows, cols >> (k + 1)), bf16) for k in range(steps)]
     slots = pltpu.VMEM((n_blk - 1, rows, width), bf16)
@@ -179,16 +208,20 @@
     vmem = pl.BlockSpec(memory_space=pltpu.VMEM)
     out = pl.pallas_call(
         functools.partial(border_kernel, n_blk, n_grp, parts),
-        out_shape=jax.ShapeDtypeStruct((n_blk, rows, cols), bf16),
+        out_shape=jax.ShapeDtypeStruct((n_blk // 2, 2, rows, cols), bf16),
         in_specs=[vmem, pl.BlockSpec(memory_space=pl.ANY), vmem],
         out_specs=vmem,
         scratch_shapes=[
-            halves, list(halves), slots, pltpu.VMEM((n_blk, rows, width), bf16), slots,
+            halves, list(halves), slots, pltpu.VMEM((n_blk // 2, 2, rows, width), bf16),
+            pltpu.VMEM((n_blk // 2, rows, width), bf16), pltpu.VMEM((n_blk // 2, rows, width), bf16),
+            pltpu.VMEM((n_blk // 2 - 1, rows, width), bf16),
             pltpu.VMEM((rows, width), bf16), pltpu.VMEM((rows, width), bf16), dma,
             dma((steps, parts)), dma((steps, parts)),
             dma((n_blk - 1, parts)), dma((n_blk - 1, parts)),
-            dma((n_blk - 1, parts)), dma((n_blk - 1, parts)),
-            dma((n_blk - 1, parts)), dma((n_blk - 1, parts)),
+            dma((n_blk // 2 - 1, parts)), dma((n_blk // 2 - 1, parts)),
+            dma((parts,)), dma((parts,)),
+            dma((n_blk // 2 - 1, parts)), dma((n_blk // 2 - 1, parts)),
+            dma((parts,)), dma((parts,)),
             dma((steps, parts)), dma((steps, parts)),
         ],
         compiler_params=pltpu.CompilerParams(

time: 66.4 us -> 65.2 us (0.982)
  Pallas kernels: 47.7 us -> 46.5 us
    pallas_call x1, Pallas kernels: 47.7 us -> 46.5 us  [border_solve(): pl.pallas_call(functools.partial(border_kernel, n_blk, n_grp, parts), out...]
where the time goes in v4:
time: 65.2 us; the launch traced here: 65 us
  Pallas kernels  46.5 us (71%)
  matrix products  15.5 us (24%)
  local copies, waits for them, and re-layouts  2.31 us (4%)
  between operations  0.73 us (1%)
    pallas_call x1, Pallas kernels, border_solve(): pl.pallas_call(functools.partial(border_kernel, n_blk, n_grp, parts), out...  46.5 us
    dot_general x1, matrix products, body(): jnp.einsum('bji,bjk->bik', block_inverse, sensitivities, preferred_elemen...  4.7 us
    dot_general x1, matrix products, body(): jnp.einsum('bji,bjk->bik', block_inverse, pulled, preferred_element_type=...  3.7 us
    dot_general x1, matrix products, body(): jnp.einsum('bmn,mk->bnk', coupling_out, full_border, preferred_element_ty...  3.65 us
    dot_general x1, matrix products, body(): jnp.einsum('bnm,bnk->mk', coupling_in, forward_half, preferred_element_ty...  3.46 us
    unnamed x14, local copies, waits for them, and re-layouts  1.62 us

profile of v4, /device:TPU:0, one launch (start us, length us, event | category | flops | bytes accessed | tf_op | source)
XLA Modules:
  0.0 65.0 jit_solution(7184983383525027809)
XLA Ops:
  0.6 0.0 copy-start
  0.7 1.6 %copy-done = bf16[2,1024,512]{2,1,0:T(8,128)(2,1)S(1)} copy-done((bf16[2,1024,512]{2,1,0:T(8,128)(2,1)S(1)}, bf16[2,1024,512]{2,1,0:T(8,128)(2,1)}, u32[]{:S(2)}) %copy-start) | copy-done | bytes 2097176
  2.2 0.0 copy-start.3
  2.2 0.0 slice-start
  2.2 4.7 %fusion.4 = f32[2,1024,512]{2,1,0:T(8,128)S(1)} fusion(bf16[2,1024,1024]{2,1,0:T(8,128)(2,1)} %param.6, bf16[2,1024,512]{2,1,0:T(8,128)(2,1)S(1)} %copy-done), kind=kOutput, calls=%fused_computation.8 | convolution fusion | flops 2147483648 | bytes 10485760 | tf_op jit(solution)/shard_map/bji,bjk->bik/dot_general | solution.py:236
  6.9 0.0 copy-done.3
  6.9 0.0 copy-start.1
  7.0 0.0 copy-start.2
  7.0 0.0 slice-start.1
  7.0 3.5 %fusion.2.flat_ref = bf16[1536,512]{1,0:T(8,128)(2,1)S(1)} fusion(bf16[2,1024,1536]{2,1,0:T(8,128)(2,1)S(1)} %copy-done.3, f32[2,1024,512]{2,1,0:T(8,128)S(1)} %fusion.4), kind=kOutput, calls=%fused_computation.4 | convolution fusion | flops 3223060480 | bytes 12058624 | tf_op jit(solution)/shard_map/bnm,bnk->mk/dot_general | solution.py:242
  10.5 0.0 copy-done.1
  10.5 0.0 copy-done.2
  10.5 46.5 %shard_map.77 = bf16[4,2,192,512]{3,2,1,0:T(8,128)(2,1)S(1)} custom-call(bf16[1536,512]{1,0:T(8,128)(2,1)S(1)} %fusion.2.flat_ref, bf16[1536,512]{1,0:T(8,128)(2,1)S(1)} %copy-done.1, bf16[192,1536]{1,0:T(8,128)(2,1)S(1)} %copy-done.2), custom_call_target="tpu_custom_call" | custom-call | tf_op jit(solution)/shard_map/pallas_call | solution.py:209
  57.0 0.7 %constant_dynamic-slice_fusion = bf16[192,512]{1,0:T(8,128)(2,1)} fusion(bf16[1536,512]{1,0:T(8,128)(2,1)S(1)} %bitcast.24, s32[]{:T(128)S(6)} %select_n.3), kind=kLoop, calls=%fused_computation.7 | loop fusion | bytes 393220 | tf_op jit(solution)/shard_map/dynamic_slice | solution.py:246
  57.7 0.0 slice-done
  57.7 0.0 slice-done.1
  57.7 0.0 copy-start.4
  57.7 3.7 %convert_bitcast_fusion = bf16[2,1024,512]{1,2,0:T(8,128)(2,1)S(1)} fusion(bf16[1536,512,1]{1,0,2:T(8,128)(2,1)S(1)} %bitcast.25, bf16[2,1536,1024]{2,1,0:T(8,128)(2,1)S(1)} %bitcast.27), kind=kOutput, calls=%fused_computation.5 | convolution fusion | flops 3222274048 | bytes 9961472 | tf_op jit(solution)/shard_map/bmn,mk->bnk/dot_general | solution.py:247
  61.3 0.0 copy-done.4
  61.3 3.7 %fusion = bf16[2,1024,512]{2,1,0:T(8,128)(2,1)} fusion(f32[2,1024,512]{2,1,0:T(8,128)S(1)} %fusion.4, bf16[2,1024,512]{1,2,0:T(8,128)(2,1)S(1)} %convert_bitcast_fusion, bf16[2,1024,1024]{2,1,0:T(8,128)(2,1)S(1)} %copy-done.4), kind=kOutput, calls=%fused_computation.1 | convolution fusion | flops 2149580800 | bytes 12582912 | tf_op jit(solution)/shard_map/bji,bjk->bik/dot_general | solution.py:251
  (1 shorter events, 0.0 us)
Async XLA Ops:
  0.6 1.6 %copy-start = (bf16[2,1024,512]{2,1,0:T(8,128)(2,1)S(1)}, bf16[2,1024,512]{2,1,0:T(8,128)(2,1)}, u32[]{:S(2)}) copy-start(bf16[2,1024,512]{2,1,0:T(8,128)(2,1)} %param.9) | copy-start | bytes 6291460
  2.2 4.7 %copy-start.3 = (bf16[2,1024,1536]{2,1,0:T(8,128)(2,1)S(1)}, bf16[2,1024,1536]{2,1,0:T(8,128)(2,1)}, u32[]{:S(2)}) copy-start(bf16[2,1024,1536]{2,1,0:T(8,128)(2,1)} %param.7) | copy-start | bytes 18874372
  2.2 55.4 %slice-start = ((s8[6291456]{0:T(1024)(128)(4,1)}), s8[4194304]{0:T(1024)(128)(4,1)S(1)}, s32[]{:S(2)}) async-start(s8[6291456]{0:T(1024)(128)(4,1)} %bitcast.26), calls=%async_computation | async-start | bytes 8388608
  6.9 3.5 %copy-start.1 = (bf16[1536,512]{1,0:T(8,128)(2,1)S(1)}, bf16[1536,512]{1,0:T(8,128)(2,1)}, u32[]{:S(2)}) copy-start(bf16[1536,512]{1,0:T(8,128)(2,1)} %rhs_hbm.1) | copy-start | bytes 4718596
  7.0 3.5 %copy-start.2 = (bf16[192,1536]{1,0:T(8,128)(2,1)S(1)}, bf16[192,1536]{1,0:T(8,128)(2,1)}, u32[]{:S(2)}) copy-start(bf16[192,1536]{1,0:T(8,128)(2,1)} %inv_ref.1) | copy-start | bytes 1769476
  7.0 50.7 %slice-start.1 = ((s8[6291456]{0:T(1024)(128)(4,1)}), s8[2097152]{0:T(1024)(128)(4,1)S(1)}, s32[]{:S(2)}) async-start(s8[6291456]{0:T(1024)(128)(4,1)} %bitcast.26), calls=%async_computation.1 | async-start | bytes 4194304
  57.7 3.7 %copy-start.4 = (bf16[2,1024,1024]{2,1,0:T(8,128)(2,1)S(1)}, bf16[2,1024,1024]{2,1,0:T(8,128)(2,1)}, u32[]{:S(2)}) copy-start(bf16[2,1024,1024]{2,1,0:T(8,128)(2,1)} %param.6) | copy-start | bytes 12582916
